TPU v7x, 32 devices: a whole 2x2x4 slice. The times are simulated.
32 devices in a mesh: front: 2 (over x), row: 4 (over y, core), col: 4 (over z).
Axes of the slice: x: 2, y: 2, z: 4, core: 2. Of those that a mesh axis runs over, the one named last changes fastest.
Arguments:
- parent: bfloat16 [49152, 1024], P(('front', 'row'), 'col'), parts along dimension 0, may hold values from -6 to 6
- contrib: bfloat16 [896, 256, 256], P(('front', 'row', 'col')), parts along dimension 0, may hold values from -6 to 6
- owner: int32 [896, 1], P(('front', 'row', 'col')), parts along dimension 0, may hold values from 0 to 15; in each aligned block of 28 rows (0 to 27, 28 to 55, ...) at most 2 rows name the same one
- slot: int32 [896], P(('front', 'row', 'col')), parts along dimension 0, may hold values from 0 to 23
- pivot: float32 [512, 256], P(('front', 'row', 'col')), parts along dimension 0, as said below
- u_factor: bfloat16 [49152, 64], P(('front', 'row', 'col')), parts along dimension 0, may hold values from -1.5 to 1.5
- v_factor: bfloat16 [49152, 64], P(('front', 'row', 'col')), parts along dimension 0, may hold values from -6 to 6
- rank: int32 [192], P(('front', 'row', 'col')), parts along dimension 0, may hold values from 8 to 64
Outputs:
- schur: float32 [49152, 1024], P(('front', 'row'), 'col'), parts along dimension 0
There are 2 independent parts, one for each index of `front`. A program takes and returns all parts, laid end to end along the dimension named above; each array names one. Nothing has to cross between parts.
Inputs may be any that keep to these rules, and one draw needn't show every extreme that they name: Among the 28 blocks of one device at most 2 name one owner, a bound that some block reaches. `pivot`: Symmetric; each diagonal entry exceeds the sum of the magnitudes of the other entries of its row.
All inputs are finite; a program needn't handle non-finite values.
Results may differ from a plain program's by a relative error of at most 0.0005.
Values may be sent and summed in bfloat16 or wider, within the bound.
A program may use at most 128 MiB of HBM per device.

v0:
```python
import jax
import jax.numpy as jnp
from jax import lax
from jax.sharding import PartitionSpec as P


def schur_complement_term(u_rows, g_rows, upper_columns, g_cols, block):
    count = u_rows.shape[0]
    width = upper_columns.shape[0]
    middle = jnp.einsum("nbr,tbs->ntrs", g_rows, g_cols, preferred_element_type=jnp.float32).astype(
        jnp.bfloat16
    )
    left_operand = jnp.einsum(
        "nbr,ntrs->ntbs", u_rows, middle, preferred_element_type=jnp.float32
    ).astype(jnp.bfloat16)
    update_term = jnp.einsum(
        "rufe,ude->rfud", left_operand, upper_columns, preferred_element_type=jnp.float32
    )
    return update_term.reshape(count * block, width * block)


def on_device(parent, contrib, owner, slot, pivot, u_factor, v_factor, rank):
    nrow = lax.axis_size("row")
    ncol = lax.axis_size("col")
    devices = nrow * ncol
    held = contrib.shape[0]
    capacity = max(2, (held + devices - 1) // devices)
    block = contrib.shape[1]
    rmax = u_factor.shape[1]
    row_block_list = parent.shape[0] // block
    wide = parent.shape[1] // block
    per_dev = rank.shape[0]
    local_count = row_block_list * wide
    target = owner[:, 0]
    hits = (target[:, None] == jnp.arange(devices)[None, :]).astype(jnp.int32)
    prior_values = jnp.cumsum(hits, axis=0) - hits
    position = jnp.sum(prior_values * hits, axis=1)
    dest = target * capacity + position
    outgoing = jnp.zeros((devices * capacity, block, block), contrib.dtype).at[dest].set(contrib)
    labels = jnp.full((devices * capacity,), -1, jnp.int32).at[dest].set(slot)
    full_pivot = lax.all_gather(pivot, ("row", "col"), axis=0, tiled=True)
    arriving_update, in_labels = (
        lax.all_to_all(outgoing, ("row", "col"), split_axis=0, concat_axis=0, tiled=True),
        lax.all_to_all(labels, ("row", "col"), split_axis=0, concat_axis=0, tiled=True),
    )
    lower = jnp.linalg.cholesky(full_pivot)
    keep = (jnp.arange(rmax)[None, :] < rank[:, None]).astype(v_factor.dtype)
    masked = v_factor.reshape(per_dev, block, rmax) * keep[:, None, :]
    rhs = masked.astype(jnp.float32).transpose(1, 0, 2).reshape(block, per_dev * rmax)
    solved = lax.linalg.triangular_solve(lower, rhs, left_side=True, lower=True)
    g_local = (
        solved.reshape(block, per_dev, rmax)
        .transpose(1, 0, 2)
        .reshape(per_dev * block, rmax)
        .astype(jnp.bfloat16)
    )
    u_every, generator_everywhere = (
        lax.all_gather(u_factor, ("row", "col"), axis=0, tiled=True),
        lax.all_gather(g_local, ("row", "col"), axis=0, tiled=True),
    )
    row_start = lax.axis_index("row") * row_block_list * block
    u_rows = lax.dynamic_slice_in_dim(u_every, row_start, row_block_list * block, 0)
    g_rows = lax.dynamic_slice_in_dim(generator_everywhere, row_start, row_block_list * block, 0)
    col_start = lax.axis_index("col") * per_dev * block
    upper_columns = lax.dynamic_slice_in_dim(u_every, col_start, wide * block, 0)
    g_cols = lax.dynamic_slice_in_dim(generator_everywhere, col_start, wide * block, 0)
    select = (in_labels[None, :] == jnp.arange(local_count)[:, None]).astype(jnp.bfloat16)
    added = jnp.dot(
        select,
        arriving_update.reshape(devices * capacity, block * block),
        preferred_element_type=jnp.float32,
    )
    added = (
        added.reshape(row_block_list, wide, block, block)
        .transpose(0, 2, 1, 3)
        .reshape(row_block_list * block, wide * block)
    )
    summed = parent.astype(jnp.float32) + added
    update_term = schur_complement_term(
        u_rows.reshape(row_block_list, block, rmax),
        g_rows.reshape(row_block_list, block, rmax),
        upper_columns.reshape(wide, block, rmax),
        g_cols.reshape(wide, block, rmax),
        block,
    )
    return summed - update_term


def solution(mesh):
    in_specs = (
        P(("front", "row"), "col"),
        P(("front", "row", "col"), None, None),
        P(("front", "row", "col"), None),
        P(("front", "row", "col")),
        P(("front", "row", "col"), None),
        P(("front", "row", "col"), None),
        P(("front", "row", "col"), None),
        P(("front", "row", "col")),
    )
    out_specs = P(("front", "row"), "col")
    return jax.shard_map(
        on_device, mesh=mesh, in_specs=in_specs, out_specs=out_specs, check_vma=False
    )
```

profile of v0, /device:TPU:13, one launch (start us, length us, event | category | flops | bytes accessed | tf_op | source)
XLA Modules:
  0.0 286.8 jit_solution(4646604598660383729)
XLA Ops:
  7.3 1.1 fusion.10
  8.5 28.4 %all_gather.10 = f32[256,256]{1,0:T(8,128)S(1)} all-gather(f32[16,256]{1,0:T(8,128)} %param.12), channel_id=1, replica_groups=mesh['front'=2,'row'=4,'col'=4] {'row','col'}, dimensions={0}, use_global_device_ids=true | all-gather | bytes 278528 | tf_op jit(solution)/shard_map/all_gather | solution.py:41
  37.1 11.7 %cholesky.50 = f32[128,128]{1,0:T(8,128)S(1)} custom-call(f32[128,128]{1,0:T(8,128)S(1)} %cholesky.118), custom_call_target="Cholesky" | custom-call | tf_op jit(solution)/shard_map/jit(cholesky)/cholesky | solution.py:46
  48.9 9.8 %custom-call.14 = f32[1,128,128]{1,2,0:T(8,128)S(1)} custom-call(f32[1,128,128]{2,1,0:T(8,128)S(1)} %get-tuple-element.28), custom_call_target="InvertDiagBlocksLowerTriangular" | custom-call | tf_op jit(solution)/shard_map/jit(cholesky)/cholesky | solution.py:46
  59.2 11.7 %cholesky.105 = f32[128,128]{1,0:T(8,128)S(1)} custom-call(f32[128,128]{1,0:T(8,128)S(1)} %convolution_subtract_fusion.1), custom_call_target="Cholesky" | custom-call | tf_op jit(solution)/shard_map/jit(cholesky)/cholesky | solution.py:46
  73.0 4.2 %while.1 = (s32[]{:T(128)}, f32[256,256]{1,0:T(8,128)S(1)}, s32[2,2]{1,0:T(2,128)S(1)}, f32[2,128,128]{2,1,0:T(8,128)S(1)}, s32[]{:T(128)}) while((s32[]{:T(128)}, f32[256,256]{1,0:T(8,128)S(1)}, s32[2,2]{1,0:T(2,128)S(1)}, f32[2,128,128]{2,1,0:T(8,128)S(1)}, s32[]{:T(128)}) %tuple.25), condition=%wide.while_cond, body=%wide.while_body.sunk | while | flops 2 | bytes 131189 | solution.py:50
  73.9 1.3 bitcast_dynamic-update-slice_fusion.2
  75.9 1.3 bitcast_dynamic-update-slice_fusion.2
  77.2 19.7 %custom-call.15 = f32[2,128,128]{1,2,0:T(8,128)S(1)} custom-call(f32[2,128,128]{2,1,0:T(8,128)S(1)} %get-tuple-element.12), custom_call_target="InvertDiagBlocksLowerTriangular" | custom-call | tf_op jit(solution)/shard_map/triangular_solve | solution.py:50
  99.2 0.8 scatter_custom_fusion
  100.6 10.4 %all-to-all-start = ((s32[16,2,1]{1,2,0:T(1,128)}), s32[16,2,1]{1,2,0:T(1,128)S(1)}, u32[]{:S(2)}, u32[]{:S(2)}) async-start(s32[16,2,1]{1,2,0:T(1,128)} %bitcast.3), calls=%async_computation | async-start | bytes 16384 | tf_op jit(solution)/shard_map/all_to_all | solution.py:44
  111.1 2.5 broadcast_in_dim.7
  113.6 10.9 %scatter_fusion = bf16[32,256,256]{2,1,0:T(8,128)(2,1)} fusion(bf16[32,256,256]{2,1,0:T(8,128)(2,1)} %broadcast_in_dim.7, s32[28]{0:T(128)S(1)} %fusion.26, bf16[28,256,256]{2,1,0:T(8,128)(2,1)} %param.9), kind=kCustom, calls=%fused_computation.1 | custom fusion | bytes 11010160 | tf_op jit(solution)/shard_map/scatter | solution.py:39
  124.5 6.1 %all-to-all-start.1 = ((bf16[32,256,256]{2,1,0:T(8,128)(2,1)}), bf16[32,256,256]{2,1,0:T(8,128)(2,1)}, u32[]{:S(2)}, u32[]{:S(2)}) async-start(bf16[32,256,256]{2,1,0:T(8,128)(2,1)} %scatter_fusion), calls=%async_computation.1 | async-start | bytes 8388608 | tf_op jit(solution)/shard_map/all_to_all | solution.py:43
  132.6 40.6 %all-gather.5.cloned.1.call-done = bf16[24576,64]{0,1:T(8,128)(2,1)} async-done(((bf16[1536,64]{0,1:T(8,128)(2,1)}), bf16[24576,64]{0,1:T(8,128)(2,1)}) %all-gather.5.cloned.1.call-update) | async-done | bytes 3145744 | tf_op jit(solution)/shard_map/all_gather | solution.py:59
  173.3 1.2 constant_dynamic-slice_fusion.2
  174.4 1.3 fusion.2
  175.7 74.9 %all-gather.3.cloned.1.call-done = bf16[24576,64]{0,1:T(8,128)(2,1)} async-done(((bf16[1536,64]{0,1:T(8,128)(2,1)}), bf16[24576,64]{0,1:T(8,128)(2,1)}) %all-gather.3.cloned.1.call-update) | async-done | bytes 3145744 | tf_op jit(solution)/shard_map/all_gather | solution.py:58
  250.6 1.2 constant_dynamic-slice_fusion.1
  251.8 4.6 %fusion.1 = f32[256,24,256]{0,2,1:T(8,128)} fusion(bf16[24,64,64]{1,2,0:T(8,128)(2,1)S(1)} %fusion.2, bf16[8,24,8,256]{3,2,1,0:T(8,128)(2,1)S(1)} %bitcast.102, bf16[24576,64]{0,1:T(8,128)(2,1)} %all-gather.3.cloned.1.call-done, s32[]{:T(128)S(6)} %select_n.18), kind=kOutput, calls=%fused_computation.7 | convolution fusion | flops 252051456 | bytes 7307268 | tf_op jit(solution)/shard_map/rufe,ude->rfud/dot_general | solution.py:16
  256.4 4.6 %copy.41 = bf16[4,8,256,256]{3,1,2,0:T(8,128)(2,1)S(1)} copy(bf16[4,8,256,256]{3,2,1,0:T(8,128)(2,1)} %bitcast.44) | data formatting | bytes 8388608
  261.0 3.7 %fusion.21 = f32[24,65536]{1,0:T(8,128)} fusion(bf16[32,65536]{1,0:T(8,128)(2,1)S(1)} %bitcast.100, s32[32]{0:T(128)S(1)} %eq.34), kind=kOutput, calls=%fused_computation.45 | convolution fusion | flops 100664064 | bytes 10485888 | tf_op jit(solution)/shard_map/dot_general | solution.py:68
  264.6 7.0 %reshape_transpose_reshape.3 = f32[6144,256]{1,0:T(8,128)} reshape(f32[24,65536]{1,0:T(8,128)} %fusion.21) | data formatting | bytes 12582912 | tf_op jit(solution)/shard_map/reshape;transpose;reshape | solution.py:76
  271.6 8.3 %bitcast_subtract_fusion = f32[6144,256]{1,0:T(8,128)} fusion(f32[256,24,256]{0,2,1:T(8,128)} %fusion.1, f32[6144,256]{1,0:T(8,128)} %reshape_transpose_reshape.3, bf16[6144,256]{1,0:T(8,128)(2,1)S(1)} %copy-done), kind=kLoop, calls=%fused_computation.4 | loop fusion | flops 4718592 | bytes 22020096 | tf_op jit(solution)/shard_map/sub | solution.py:86
  (45 shorter events, 8.7 us)
Async XLA Ops:
  6.5 166.7 %all-gather.5.cloned.1.call-start = ((), (), s32[]{:S(2)}) async-start(), calls=%async_computation.3 | async-start | bytes 3342336 | tf_op jit(solution)/shard_map/all_gather | solution.py:59
  7.3 91.6 %copy-start.1 = (s32[28,1]{0,1:T(1,128)S(1)}, s32[28,1]{0,1:T(1,128)}, u32[]{:S(2)}) copy-start(s32[28,1]{0,1:T(1,128)} %param.10) | copy-start | bytes 340
  100.6 23.8 %all-to-all-start = ((s32[16,2,1]{1,2,0:T(1,128)}), s32[16,2,1]{1,2,0:T(1,128)S(1)}, u32[]{:S(2)}, u32[]{:S(2)}) async-start(s32[16,2,1]{1,2,0:T(1,128)} %bitcast.3), calls=%async_computation | async-start | bytes 16384 | tf_op jit(solution)/shard_map/all_to_all | solution.py:44
  124.5 131.9 %all-to-all-start.1 = ((bf16[32,256,256]{2,1,0:T(8,128)(2,1)}), bf16[32,256,256]{2,1,0:T(8,128)(2,1)}, u32[]{:S(2)}, u32[]{:S(2)}) async-start(bf16[32,256,256]{2,1,0:T(8,128)(2,1)} %scatter_fusion), calls=%async_computation.1 | async-start | bytes 8388608 | tf_op jit(solution)/shard_map/all_to_all | solution.py:43
  130.5 120.0 %all-gather.3.cloned.1.call-start = ((), (), s32[]{:S(2)}) async-start(), calls=%async_computation.2 | async-start | bytes 3342336 | tf_op jit(solution)/shard_map/all_gather | solution.py:58
  264.6 7.0 %copy-start = (bf16[6144,256]{1,0:T(8,128)(2,1)S(1)}, bf16[6144,256]{1,0:T(8,128)(2,1)}, u32[]{:S(2)}) copy-start(bf16[6144,256]{1,0:T(8,128)(2,1)} %param.8) | copy-start | bytes 9437188
Sparse Core Ops, SparseCore 0:
  98.9 74.2 all-gather.4
  175.6 74.9 all-gather.2
where the time goes:
time: 291 us; the launch traced here: 287 us
  waiting for transfers between devices  116 us (40%)
  other arithmetic  64.9 us (22%)
  local copies, waits for them, and re-layouts  34.7 us (12%)
  blocking collectives  28.4 us (10%)
  starting transfers between devices  16.6 us (6%)
  between operations  14.8 us (5%)
  matrix products  11 us (4%)
    all_gather x1, waiting for transfers between devices, on_device(): lax.all_gather(u_factor, ('row', 'col'), axis=0, tiled=True)  74.9 us
    all_gather x1, waiting for transfers between devices, on_device(): lax.all_gather(g_local, ('row', 'col'), axis=0, tiled=True)  40.6 us
    another operation x6, other arithmetic, on_device(): lower = jnp.linalg.cholesky(full_pivot)  34 us
    all_gather x1, blocking collectives, on_device(): full_pivot = lax.all_gather(pivot, ('row', 'col'), axis=0, tiled=True)  28.4 us
    another operation x5, other arithmetic, on_device(): solved = lax.linalg.triangular_solve(lower, rhs, left_side=True, lower=True)  19.8 us
    scatter x1, local copies, waits for them, and re-layouts, on_device(): jnp.zeros((devices * capacity, block, block), contrib.dtype).at[dest]  10.9 us
    all_to_all x1, starting transfers between devices, on_device(): lax.all_to_all(labels, ('row', 'col'), split_axis=0, concat_axis=0, tiled...  10.4 us
    sub x1, other arithmetic, on_device(): return summed - update_term  8.32 us
  transfers between devices with their start and end apart: 4, of which 2 were waited for; matrix products, arithmetic and copies ran while one was open for 8% of the time, Pallas kernels for 0%

commit v1 on v0

v1 whole, which is shorter than its diff:
```python
import functools

import jax
import jax.numpy as jnp
from jax import lax
from jax.experimental import pallas as pl
from jax.experimental.pallas import tpu as pltpu
from jax.sharding import PartitionSpec as P

MESH = pl.DeviceIdType.MESH
F32 = jnp.float32
BF16 = jnp.bfloat16


def exact_dot(a, b, contract):
    return lax.dot_general(
        a, b, (contract, ((), ())), precision=lax.Precision.HIGHEST, preferred_element_type=F32
    )


def inverse_factor(work):
    size = work.shape[0]
    rows = lax.broadcasted_iota(jnp.int32, (size, size), 0)
    lanes = lax.broadcasted_iota(jnp.int32, (size, size), 1)
    one_lane = lax.broadcasted_iota(jnp.int32, (1, size), 1)

    def step(k, carry):
        m = work[...]
        top = work[pl.ds(k, 1), :]
        pivot = jnp.sum(jnp.where(one_lane == k, top, 0.0), axis=1, keepdims=True)
        root = lax.rsqrt(pivot)
        root = root * (1.5 - 0.5 * pivot * root * root)
        column = jnp.sum(jnp.where(lanes == k, m, 0.0), axis=1, keepdims=True)
        scaled = jnp.where(one_lane == k, 1.0, top) * root
        factor = column * root
        below = jnp.where(lanes == k, 0.0, m) - factor * scaled
        work[...] = jnp.where(rows > k, below, jnp.where(rows == k, scaled, m))
        return carry

    lax.fori_loop(0, size, step, 0)
    work[...] = jnp.where(lanes <= rows, work[...], 0.0)


def split3(x):
    hi = x.astype(BF16)
    rest = x - hi.astype(F32)
    mid = rest.astype(BF16)
    low = (rest - mid.astype(F32)).astype(BF16)
    return hi, mid, low


def solve(parts, rhs):
    hi, mid, low = (jnp.dot(p, rhs, preferred_element_type=F32) for p in parts)
    return (hi + (mid + low)).astype(BF16)


def exchange_kernel(
    nr, nc, cap, per_dev,
    src_ref, labels_ref, contrib_ref, pivot_ref, vwide_ref, vfirst_ref, upack_ref,
    arr_ref, lab_ref, uall_ref, uc_ref, mid_ref,
    pack, piv, vc, mids, work1, work2,
    blk_s, blk_r, lab_s, lab_r, piv_s, piv_r, vc_s, vc_r, uc_s, uc_r, u_s, u_r, mid_s, mid_r, loc,
):
    n = nr * nc
    r = lax.axis_index("row")
    c = lax.axis_index("col")
    me = r * nc + c
    prows = pivot_ref.shape[0]
    half = vfirst_ref.shape[0]
    block = 2 * half
    rmax = vfirst_ref.shape[1] // 2

    def peer(s):
        return lax.rem(r + s // nc, nr), lax.rem(c + s % nc, nc)

    def flip(m):
        return c + m - 2 * m * lax.rem(c // m, 2)

    def remote(src, dst, ssem, rsem, rr, cc):
        return pltpu.make_async_remote_copy(
            src_ref=src, dst_ref=dst, send_sem=ssem, recv_sem=rsem,
            device_id={"row": rr, "col": cc}, device_id_type=MESH,
        )

    barrier = pltpu.get_barrier_semaphore()
    for s in range(1, n):
        rr, cc = peer(s)
        pl.semaphore_signal(barrier, inc=1, device_id={"row": rr, "col": cc}, device_id_type=MESH)
    pl.semaphore_wait(barrier, n - 1)

    order = sorted(range(1, n), key=lambda s: (min(s % nc, nc - s % nc) * -1, s // nc))

    pivot_copies, first_copies = [], []
    my_piv = piv.at[pl.ds(pl.multiple_of(me * prows, prows), prows)]
    for s in order:
        rr, cc = peer(s)
        copy = remote(pivot_ref, my_piv, piv_s.at[s], piv_r.at[s], rr, cc)
        copy.start()
        pivot_copies.append(copy)
    for s in order:
        rr, cc = peer(s)
        copy = remote(vfirst_ref, vc.at[c], vc_s.at[s], vc_r.at[s], rr, cc)
        pl.when(r == 0)(copy.start)
        first_copies.append((s, copy))
    column_copies = []
    for s in range(nc, n, nc):
        rr, cc = peer(s)
        copy = remote(upack_ref.at[pl.ds(0, half)], uc_ref, uc_s.at[s], uc_r.at[s], rr, cc)
        pl.when(r == 0)(copy.start)
        column_copies.append((s, copy))

    locals_ = [
        pltpu.make_async_copy(pivot_ref, my_piv, loc.at[0]),
        pltpu.make_async_copy(upack_ref, uall_ref.at[c], loc.at[1]),
        pltpu.make_async_copy(labels_ref.at[me], lab_ref.at[me], loc.at[2]),
    ]
    for copy in locals_:
        copy.start()
    own_v = pltpu.make_async_copy(vfirst_ref, vc.at[c], loc.at[3])
    own_u = pltpu.make_async_copy(upack_ref.at[pl.ds(0, half)], uc_ref, loc.at[4])

    @pl.when(r == 0)
    def _():
        own_v.start()
        own_u.start()

    masks = []
    m = nc // 2
    while m:
        masks.append(m)
        m //= 2
    u_copies, stage, sem = [], [], 0
    held = [[]]
    for m in masks:
        stage.append([(m, path, sem + q) for q, path in enumerate(held)])
        sem += len(held)
        held = held + [path + [m] for path in held]

    def start_stage(entries):
        for m, path, q in entries:
            origin = c
            for step in path:
                origin = origin + step - 2 * step * lax.rem(c // step, 2)
            source = upack_ref if not path else uall_ref.at[origin]
            copy = remote(source, uall_ref.at[origin], u_s.at[q], u_r.at[q], r, flip(m))
            copy.start()
            u_copies.append(copy)

    start_stage(stage[0])

    block_copies = []
    for s in order + [0]:
        rr, cc = peer(s)
        target = rr * nc + cc
        for k in range(cap):
            pack[s * cap + k] = contrib_ref[src_ref[target * cap + k]]
        mine = arr_ref.at[pl.ds(me * cap, cap)]
        packed = pack.at[pl.ds(s * cap, cap)]
        if s:
            copy = remote(packed, mine, blk_s.at[s], blk_r.at[s], rr, cc)
            copy.start()
            block_copies.append(copy)
            copy = remote(labels_ref.at[target], lab_ref.at[me], lab_s.at[s], lab_r.at[s], rr, cc)
            copy.start()
            block_copies.append(copy)
        else:
            copy = pltpu.make_async_copy(packed, mine, loc.at[5])
            copy.start()
            locals_.append(copy)

    locals_[0].wait()
    for copy in pivot_copies:
        copy.wait()

    work1[...] = piv[0:half, 0:half]
    inverse_factor(work1)
    inv1 = work1[...]
    low = exact_dot(piv[half:, 0:half], inv1, ((1,), (1,)))
    work2[...] = piv[half:, half:] - exact_dot(low, low, ((1,), (1,)))

    sent = 0
    for entries in stage[1:]:
        for copy in u_copies[sent:]:
            copy.wait_recv()
        sent = len(u_copies)
        start_stage(entries)

    inverse_factor(work2)
    inv2 = work2[...]
    inv21 = -exact_dot(inv2, exact_dot(low, inv1, ((1,), (0,))), ((1,), (0,)))
    inverse = jnp.concatenate(
        [
            jnp.concatenate([inv1, jnp.zeros_like(inv1)], axis=1),
            jnp.concatenate([inv21, inv2], axis=1),
        ],
        axis=0,
    )
    parts = split3(inverse)
    g_own = solve(parts, vwide_ref[...])

    @pl.when(r == 0)
    def _():
        own_v.wait()
        own_u.wait()

    for s, copy in first_copies:
        pl.when(r == 0)(copy.wait_send)
        pl.when(lax.rem(r + nr - s // nc, nr) == 0)(copy.wait_recv)

    mid_copies = []
    for t in range(nc):
        packed_v = vc[t]
        v_t = jnp.concatenate([packed_v[:, :rmax], packed_v[:, rmax:]], axis=0)
        g_t = solve(parts, v_t)
        middle = lax.dot_general(
            g_own, g_t, (((0,), (0,)), ((), ())), preferred_element_type=F32
        ).astype(BF16)
        for j in range((per_dev + 1) // 2):
            first = middle[2 * j * rmax : (2 * j + 1) * rmax]
            if 2 * j + 1 < per_dev:
                second = middle[(2 * j + 1) * rmax : (2 * j + 2) * rmax]
            else:
                second = jnp.zeros_like(first)
            mids[t, j * rmax : (j + 1) * rmax] = jnp.concatenate([first, second], axis=1)
    for s in range(1, nc):
        cc = lax.rem(c + s, nc)
        copy = remote(mids.at[cc], mid_ref.at[c], mid_s.at[s], mid_r.at[s], r, cc)
        copy.start()
        mid_copies.append(copy)
    copy = pltpu.make_async_copy(mids.at[c], mid_ref.at[c], loc.at[6])
    copy.start()
    locals_.append(copy)

    for copy in locals_[1:]:
        copy.wait()
    for s, copy in column_copies:
        pl.when(r == 0)(copy.wait_send)
        pl.when(lax.rem(r + nr - s // nc, nr) == 0)(copy.wait_recv)
    for copy in u_copies[:sent]:
        copy.wait_send()
    for copy in u_copies[sent:]:
        copy.wait()
    for copy in mid_copies + block_copies:
        copy.wait()


def update_kernel(cap, per_dev, lab_ref, parent_ref, arr_ref, u_ref, mid_ref, uc_ref, out_ref, head, nxt):
    step = pl.program_id(0)
    slots = arr_ref.shape[0]
    block = arr_ref.shape[1]
    half = u_ref.shape[2]
    rmax = half // 2

    @pl.when(step == 0)
    def _():
        for i in range(head.shape[0]):
            head[i] = -1

        def link(j, carry):
            label = lab_ref[j // cap, 0, lax.rem(j, cap)]

            @pl.when(label >= 0)
            def _():
                nxt[j] = head[label]
                head[label] = j

            return carry

        lax.fori_loop(0, slots, link, 0)

    uc = uc_ref[...]
    top, bottom = uc[:, :rmax], uc[:, rmax:]
    right = jnp.concatenate([top, bottom], axis=0)
    zero = jnp.zeros_like(right)
    right_top = jnp.concatenate([right, zero], axis=1)
    right_bottom = jnp.concatenate([zero, right], axis=1)
    for i in range(per_dev):
        j = i // 2
        middle = mid_ref[0, j * rmax : (j + 1) * rmax, (i % 2) * rmax : (i % 2 + 1) * rmax]
        blank = jnp.zeros_like(middle)
        spread = jnp.concatenate(
            [jnp.concatenate([middle, blank], axis=1), jnp.concatenate([blank, middle], axis=1)], axis=0
        )
        left = jnp.dot(
            u_ref[0, i * half : (i + 1) * half], spread, preferred_element_type=F32
        ).astype(BF16)
        rows = pl.ds(i * block, half)
        later = pl.ds(i * block + half, half)
        out_ref[rows] = parent_ref[rows].astype(F32) - lax.dot_general(
            left, right_top, (((1,), (1,)), ((), ())), preferred_element_type=F32
        )
        out_ref[later] = parent_ref[later].astype(F32) - lax.dot_general(
            left, right_bottom, (((1,), (1,)), ((), ())), preferred_element_type=F32
        )

        def add(j):
            out_ref[pl.ds(i * block, block)] += arr_ref[j].astype(F32)
            return nxt[j]

        lax.while_loop(lambda j: j >= 0, add, head[step * per_dev + i])


def on_device(parent, contrib, owner, slot, pivot, u_factor, v_factor, rank):
    nr = lax.axis_size("row")
    nc = lax.axis_size("col")
    n = nr * nc
    held, block, _ = contrib.shape
    cap = max(2, (held + n - 1) // n)
    rmax = u_factor.shape[1]
    per_dev = rank.shape[0]
    half = block // 2
    pairs = (per_dev + 1) // 2
    local_count = parent.shape[0] // block

    target = owner[:, 0]
    index = jnp.arange(held)
    earlier = (target[None, :] == target[:, None]) & (index[None, :] < index[:, None])
    dest = target * cap + jnp.sum(earlier, axis=1)
    hit = dest[None, :] == jnp.arange(n * cap)[:, None]
    source = jnp.sum(jnp.where(hit, index[None, :], 0), axis=1).astype(jnp.int32)
    label = (jnp.sum(jnp.where(hit, slot[None, :] + 1, 0), axis=1) - 1).astype(jnp.int32)
    labels = jnp.pad(label.reshape(n, 1, cap), ((0, 0), (0, 0), (0, 128 - cap)))

    keep = jnp.arange(rmax)[None, :] < rank[:, None]
    masked = jnp.where(keep[:, None, :], v_factor.reshape(per_dev, block, rmax), 0)
    v_wide = masked.transpose(1, 0, 2).reshape(block, per_dev * rmax)
    v_first = masked[0].reshape(2, half, rmax).transpose(1, 0, 2).reshape(half, 2 * rmax)
    u_pack = (
        u_factor.reshape(per_dev, 2, half, rmax).transpose(0, 2, 1, 3).reshape(per_dev * half, 2 * rmax)
    )

    dma = pltpu.SemaphoreType.DMA
    vmem = pl.BlockSpec(memory_space=pltpu.VMEM)
    anywhere = pl.BlockSpec(memory_space=pl.ANY)
    arrived, in_labels, u_all, u_col, mids = pl.pallas_call(
        functools.partial(exchange_kernel, nr, nc, cap, per_dev),
        out_shape=(
            jax.ShapeDtypeStruct((n * cap, block, block), contrib.dtype),
            jax.ShapeDtypeStruct((n, 1, 128), jnp.int32),
            jax.ShapeDtypeStruct((nc, per_dev * half, 2 * rmax), BF16),
            jax.ShapeDtypeStruct((half, 2 * rmax), BF16),
            jax.ShapeDtypeStruct((nc, pairs * rmax, 2 * rmax), BF16),
        ),
        in_specs=[
            pl.BlockSpec(memory_space=pltpu.SMEM), anywhere, vmem, vmem, vmem, vmem, anywhere,
        ],
        out_specs=(anywhere,) * 5,
        scratch_shapes=[
            pltpu.VMEM((n * cap, block, block), contrib.dtype),
            pltpu.VMEM((block, block), F32),
            pltpu.VMEM((nc, half, 2 * rmax), BF16),
            pltpu.VMEM((nc, pairs * rmax, 2 * rmax), BF16),
            pltpu.VMEM((half, half), F32),
            pltpu.VMEM((half, half), F32),
        ]
        + [dma((n,))] * 10
        + [dma((nc,))] * 4
        + [dma((7,))],
        compiler_params=pltpu.CompilerParams(
            collective_id=0, has_side_effects=True, vmem_limit_bytes=32 << 20
        ),
    )(source, labels, contrib, pivot, v_wide, v_first, u_pack)

    span = per_dev * block
    return pl.pallas_call(
        functools.partial(update_kernel, cap, per_dev),
        grid=(local_count // per_dev,),
        out_shape=jax.ShapeDtypeStruct(parent.shape, F32),
        in_specs=[
            pl.BlockSpec(memory_space=pltpu.SMEM),
            pl.BlockSpec((span, block), lambda i: (i, 0)),
            pl.BlockSpec((n * cap, block, block), lambda i: (0, 0, 0)),
            pl.BlockSpec((1, per_dev * half, 2 * rmax), lambda i: (i, 0, 0)),
            pl.BlockSpec((1, pairs * rmax, 2 * rmax), lambda i: (i, 0, 0)),
            pl.BlockSpec((half, 2 * rmax), lambda i: (0, 0)),
        ],
        out_specs=pl.BlockSpec((span, block), lambda i: (i, 0)),
        scratch_shapes=[pltpu.SMEM((local_count,), jnp.int32), pltpu.SMEM((n * cap,), jnp.int32)],
        compiler_params=pltpu.CompilerParams(vmem_limit_bytes=40 << 20),
    )(in_labels, parent, arrived, u_all, mids, u_col)


def solution(mesh):
    in_specs = (
        P(("front", "row"), "col"),
        P(("front", "row", "col"), None, None),
        P(("front", "row", "col"), None),
        P(("front", "row", "col")),
        P(("front", "row", "col"), None),
        P(("front", "row", "col"), None),
        P(("front", "row", "col"), None),
        P(("front", "row", "col")),
    )
    return jax.shard_map(
        on_device, mesh=mesh, in_specs=in_specs, out_specs=P(("front", "row"), "col"), check_vma=False
    )
```

time: 291 us -> 150 us (0.52)
  the two profiles are of different devices: /device:TPU:13 before, /device:TPU:0 now
where the time goes in v1:
time: 150 us
  Pallas kernels  136 us (91%)
  local copies, waits for them, and re-layouts  9.55 us (6%)
  other arithmetic  5.14 us (3%)
    pallas_call x1, Pallas kernels, on_device(): pl.pallas_call(functools.partial(exchange_kernel, nr, nc, cap, per_dev),...  123 us
    pallas_call x1, Pallas kernels, on_device(): pl.pallas_call(functools.partial(update_kernel, cap, per_dev), grid=(loca...  12.1 us
    unnamed x9, local copies, waits for them, and re-layouts  3.54 us

profile of v1, /device:TPU:0, one launch (start us, length us, event | category | flops | bytes accessed | tf_op | source)
XLA Modules:
  0.0 150.3 jit_solution(13776632525695525934)
XLA Ops:
  0.0 0.9 convert_reduce_fusion
  0.9 0.7 multiply_add_fusion
  1.6 0.1 select_reduce_fusion
  1.7 0.1 sub.7
  1.8 1.3 iota_compare_fusion
  3.1 0.0 copy-start.1
  3.1 1.1 reshape.59
  4.3 0.2 copy.25.upack_ref
  4.5 1.9 %reshape.56 = bf16[6,256,64]{1,0,2:T(8,128)(2,1)} reshape(bf16[1536,64]{0,1:T(8,128)(2,1)} %param.14) | data formatting | bytes 393216 | tf_op jit(solution)/shard_map/reshape | solution.py:325
  6.3 1.1 fusion.1
  7.4 0.7 copy.20
  8.1 1.1 broadcast_select_fusion
  9.2 0.2 slice_reduce_fusion
  9.4 0.7 copy.24.vfirst_ref
  10.2 1.1 copy.23.vwide_ref
  11.2 0.0 copy-start
  11.3 2.0 %copy-done = bf16[28,256,256]{2,1,0:T(8,128)(2,1)S(1)} copy-done((bf16[28,256,256]{2,1,0:T(8,128)(2,1)S(1)}, bf16[28,256,256]{2,1,0:T(8,128)(2,1)}, u32[]{:S(2)}) %copy-start) | copy-done | bytes 3670040
  13.3 0.0 copy-start.2
  13.3 0.8 copy-done.2
  14.0 0.0 copy-start.3
  14.0 0.7 copy-done.3
  14.8 123.4 %shard_map.82 = (bf16[32,256,256]{2,1,0:T(8,128)(2,1)S(1)}, s32[16,1,128]{2,1,0:T(1,128)S(1)}, bf16[4,768,128]{2,1,0:T(8,128)(2,1)S(1)}, bf16[128,128]{1,0:T(8,128)(2,1)S(1)}, bf16[4,192,128]{2,1,0:T(8,128)(2,1)S(1)}) custom-call(s32[32]{0:T(128)S(1)} %get-tuple-element.16.src_ref, s32[16,1,128]{2,1,0:T(1,128)S(1)} %pad.4.labels_ref, ...), custom_call_target="tpu_custom_call" | custom-call | tf_op jit(solution)/shard_map/pallas_call | solution.py:335
  138.2 0.0 copy-done.1
  138.2 12.1 %shard_map.83 = f32[6144,256]{1,0:T(8,128)} custom-call(s32[16,1,128]{2,1,0:T(1,128)S(1)} %get-tuple-element.10.lab_ref, bf16[6144,256]{1,0:T(8,128)(2,1)S(1)} %copy-done.1, bf16[32,256,256]{2,1,0:T(8,128)(2,1)S(1)} %get-tuple-element.11.arr_ref, bf16[4,768,128]{2,1,0:T(8,128)(2,1)S(1)} %get-tuple-element.12.u_ref, ...), custom_call_target="tpu_custom_call" | custom-call | tf_op jit(solution)/shard_map/pallas_call | solution.py:365
  (6 shorter events, 0.1 us)
Async XLA Ops:
  3.1 135.1 %copy-start.1 = (bf16[6144,256]{1,0:T(8,128)(2,1)S(1)}, bf16[6144,256]{1,0:T(8,128)(2,1)}, u32[]{:S(2)}) copy-start(bf16[6144,256]{1,0:T(8,128)(2,1)} %parent_ref.1) | copy-start | bytes 9437188
  11.2 2.0 %copy-start = (bf16[28,256,256]{2,1,0:T(8,128)(2,1)S(1)}, bf16[28,256,256]{2,1,0:T(8,128)(2,1)}, u32[]{:S(2)}) copy-start(bf16[28,256,256]{2,1,0:T(8,128)(2,1)} %contrib_ref.1) | copy-start | bytes 11010052
  13.3 0.8 copy-start.2
  14.0 0.7 copy-start.3

commit v2 on v1

v2 whole, which is shorter than its diff:
```python
import functools

import jax
import jax.numpy as jnp
from jax import lax
from jax.experimental import pallas as pl
from jax.experimental.pallas import tpu as pltpu
from jax.sharding import PartitionSpec as P

MESH = pl.DeviceIdType.MESH
F32 = jnp.float32
BF16 = jnp.bfloat16
EARLY = 9


def exact_dot(a, b, contract):
    return lax.dot_general(
        a, b, (contract, ((), ())), precision=lax.Precision.HIGHEST, preferred_element_type=F32
    )


def inverse_factor(work):
    size = work.shape[0]
    rows = lax.broadcasted_iota(jnp.int32, (size, size), 0)
    lanes = lax.broadcasted_iota(jnp.int32, (size, size), 1)
    one_lane = lax.broadcasted_iota(jnp.int32, (1, size), 1)

    def step(k, carry):
        m = work[...]
        top = work[pl.ds(k, 1), :]
        pivot = jnp.sum(jnp.where(one_lane == k, top, 0.0), axis=1, keepdims=True)
        root = lax.rsqrt(pivot)
        root = root * (1.5 - 0.5 * pivot * root * root)
        column = jnp.sum(jnp.where(lanes == k, m, 0.0), axis=1, keepdims=True)
        scaled = jnp.where(one_lane == k, 1.0, top) * root
        factor = column * root
        below = jnp.where(lanes == k, 0.0, m) - factor * scaled
        work[...] = jnp.where(rows > k, below, jnp.where(rows == k, scaled, m))
        return carry

    lax.fori_loop(0, size, step, 0)
    work[...] = jnp.where(lanes <= rows, work[...], 0.0)


def split3(x):
    hi = x.astype(BF16)
    rest = x - hi.astype(F32)
    mid = rest.astype(BF16)
    low = (rest - mid.astype(F32)).astype(BF16)
    return hi, mid, low


def solve(parts, rhs_t):
    hi, mid, low = (
        lax.dot_general(rhs_t, p, (((1,), (1,)), ((), ())), preferred_element_type=F32) for p in parts
    )
    return (hi + (mid + low)).astype(BF16)


def exchange_kernel(
    nr, nc, cap, per_dev,
    owner_ref, slot_ref, rank_ref, contrib_ref, pivot_ref, vt_ref, ut_ref, parent_ref,
    arr_ref, lab_ref, base_ref,
    cbuf, pack, piv, vown, vfirst, vc, ug, uc, mid_out, mid_in, labels, par, work1, work2,
    blk_s, blk_r, lab_s, lab_r, piv1_s, piv1_r, v1_s, v1_r, u_s, u_r, mid_s, mid_r,
    piv2_s, piv2_r, v2_s, v2_r, uc_s, uc_r, loc,
):
    n = nr * nc
    r = lax.axis_index("row")
    c = lax.axis_index("col")
    me = r * nc + c
    held, block, _ = contrib_ref.shape
    prows = pivot_ref.shape[0]
    rmax = vt_ref.shape[0]
    half = block // 2

    def peer(s):
        return lax.rem(r + s // nc, nr), lax.rem(c + s % nc, nc)

    def flip(m):
        return c + m - 2 * m * lax.rem(c // m, 2)

    def remote(src, dst, ssem, rsem, rr, cc):
        return pltpu.make_async_remote_copy(
            src_ref=src, dst_ref=dst, send_sem=ssem, recv_sem=rsem,
            device_id={"row": rr, "col": cc}, device_id_type=MESH,
        )

    my_piv = piv.at[pl.ds(pl.multiple_of(me * prows, prows), prows)]
    row_piv = piv.at[pl.ds(pl.multiple_of(r * nc * prows, nc * prows), nc * prows)]
    my_vc = vc.at[pl.ds(pl.multiple_of(c * rmax, rmax), rmax)]
    first_u = ut_ref.at[:, pl.ds(0, block)]
    load_v = pltpu.make_async_copy(vt_ref, vown, loc.at[0])
    load_piv = pltpu.make_async_copy(pivot_ref, my_piv, loc.at[1])
    load_contrib = pltpu.make_async_copy(contrib_ref, cbuf, loc.at[2])
    load_u = pltpu.make_async_copy(ut_ref, ug.at[c], loc.at[3])
    load_uc = pltpu.make_async_copy(first_u, uc, loc.at[4])
    load_parent = pltpu.make_async_copy(parent_ref, par, loc.at[5])
    for copy in (load_v, load_piv, load_contrib, load_u, load_parent):
        copy.start()
    pl.when(r == 0)(load_uc.start)

    barrier = pltpu.get_barrier_semaphore()
    for s in range(1, n):
        rr, cc = peer(s)
        pl.semaphore_signal(barrier, inc=1, device_id={"row": rr, "col": cc}, device_id_type=MESH)
    load_v.wait()
    vfirst[...] = jnp.where(
        lax.broadcasted_iota(jnp.int32, (rmax, block), 0) < rank_ref[0], vown[:, 0:block], 0
    ).astype(BF16)
    pl.semaphore_wait(barrier, n - 1)

    pivot_1, pivot_2, first_1, first_2, column_u = [], [], [], [], []
    for s in range(1, nc):
        cc = lax.rem(c + s, nc)
        copy = remote(pivot_ref, my_piv, piv1_s.at[s], piv1_r.at[s], r, cc)
        copy.start()
        pivot_1.append(copy)
    for s in range(1, nc):
        cc = lax.rem(c + s, nc)
        copy = remote(vfirst, my_vc, v1_s.at[s], v1_r.at[s], r, cc)
        pl.when(r == 0)(copy.start)
        first_1.append(copy)

    masks = []
    m = nc // 2
    while m:
        masks.append(m)
        m //= 2
    u_copies, stages, sem, paths = [], [], 0, [[]]
    for m in masks:
        stages.append([(m, path, sem + q) for q, path in enumerate(paths)])
        sem += len(paths)
        paths = paths + [path + [m] for path in paths]

    def start_stage(entries):
        for m, path, q in entries:
            origin = c
            for step in path:
                origin = origin + step - 2 * step * lax.rem(c // step, 2)
            source = ug.at[origin] if path else ut_ref
            copy = remote(source, ug.at[origin], u_s.at[q], u_r.at[q], r, flip(m))
            copy.start()
            u_copies.append(copy)

    start_stage(stages[0])

    lane = lax.broadcasted_iota(jnp.int32, (1, 128), 1)

    def pack_for(s):
        rr, cc = peer(s)
        target = rr * nc + cc

        def look(j, carry):
            count, found = carry[0], carry[1:]
            hit = owner_ref[j] == target
            found = [jnp.where(hit & (count == k), j, found[k]) for k in range(cap)]
            return (jnp.where(hit, count + 1, count), *found)

        count, *found = lax.fori_loop(0, held, look, (jnp.int32(0),) * (cap + 1))
        row = jnp.full((1, 128), -1, jnp.int32)
        for k in range(cap):
            pack[s * cap + k] = cbuf[found[k]]
            row = jnp.where(lane == k, jnp.where(count > k, slot_ref[found[k]], -1), row)
        labels[s] = row

    mine = arr_ref.at[pl.ds(me * cap, cap)]
    block_copies = []

    def send(s):
        rr, cc = peer(s)
        copies = (
            remote(pack.at[pl.ds(s * cap, cap)], mine, blk_s.at[s], blk_r.at[s], rr, cc),
            remote(labels.at[s], lab_ref.at[me], lab_s.at[s], lab_r.at[s], rr, cc),
        )
        for copy in copies:
            copy.start()
            block_copies.append(copy)

    order = sorted(range(1, n), key=lambda s: (-min(s % nc, nc - s % nc), s // nc))
    early = order[: (EARLY * len(order)) // 16]
    late = order[len(early) :]
    ahead = early[: nc // 2]
    load_contrib.wait()
    for s in ahead:
        pack_for(s)

    load_piv.wait()
    for copy in pivot_1:
        copy.wait_recv()
    for s in range(1, nr):
        rr = lax.rem(r + s, nr)
        copy = remote(row_piv, row_piv, piv2_s.at[s], piv2_r.at[s], rr, c)
        copy.start()
        pivot_2.append(copy)

    @pl.when(r == 0)
    def _():
        vc[pl.ds(pl.multiple_of(c * rmax, rmax), rmax)] = vfirst[...]
        for copy in first_1:
            copy.wait_recv()

    for s in range(1, nr):
        rr = lax.rem(r + s, nr)
        copy = remote(vc, vc, v2_s.at[s], v2_r.at[s], rr, c)
        pl.when(r == 0)(copy.start)
        first_2.append((s, copy))
        copy = remote(first_u, uc, uc_s.at[s], uc_r.at[s], rr, c)
        pl.when(r == 0)(copy.start)
        column_u.append((s, copy))

    for s in ahead:
        send(s)
    for s in early[len(ahead) :]:
        pack_for(s)
        send(s)
    for s in late + [0]:
        pack_for(s)
    own = [
        pltpu.make_async_copy(pack.at[pl.ds(0, cap)], mine, loc.at[6]),
        pltpu.make_async_copy(labels.at[0], lab_ref.at[me], loc.at[7]),
    ]
    for copy in own:
        copy.start()

    for copy in pivot_2:
        copy.wait_recv()

    work1[...] = piv[0:half, 0:half]
    inverse_factor(work1)
    inv1 = work1[...]
    low = exact_dot(piv[half:, 0:half], inv1, ((1,), (1,)))
    work2[...] = piv[half:, half:] - exact_dot(low, low, ((1,), (1,)))

    sent = 0
    for entries in stages[1:]:
        for copy in u_copies[sent:]:
            copy.wait_recv()
        sent = len(u_copies)
        start_stage(entries)

    inverse_factor(work2)
    inv2 = work2[...]
    inv21 = -exact_dot(inv2, exact_dot(low, inv1, ((1,), (0,))), ((1,), (0,)))
    inverse = jnp.concatenate(
        [
            jnp.concatenate([inv1, jnp.zeros_like(inv1)], axis=1),
            jnp.concatenate([inv21, inv2], axis=1),
        ],
        axis=0,
    )
    parts = split3(inverse)
    place = lax.broadcasted_iota(jnp.int32, (rmax, block), 0)
    masked = [
        jnp.where(place < rank_ref[i], vown[:, i * block : (i + 1) * block], 0).astype(BF16)
        for i in range(per_dev)
    ]
    g_own = solve(parts, jnp.concatenate(masked, axis=0))

    for s, copy in first_2:
        pl.when(r == 0)(copy.wait_send)
        pl.when(lax.rem(r + nr - s, nr) == 0)(copy.wait_recv)
    g_columns = solve(parts, vc[...])
    mid_out[...] = lax.dot_general(
        g_columns, g_own, (((1,), (1,)), ((), ())), preferred_element_type=F32
    ).astype(BF16)
    mid_copies = []
    for s in range(1, nc):
        cc = lax.rem(c + s, nc)
        rows = mid_out.at[pl.ds(pl.multiple_of(cc * rmax, rmax), rmax)]
        copy = remote(rows, mid_in.at[c], mid_s.at[s], mid_r.at[s], r, cc)
        copy.start()
        mid_copies.append(copy)
    for s in late:
        send(s)
    mid_in[c] = mid_out[pl.ds(pl.multiple_of(c * rmax, rmax), rmax)]

    load_u.wait()
    load_parent.wait()
    pl.when(r == 0)(load_uc.wait)
    for s, copy in column_u:
        pl.when(r == 0)(copy.wait_send)
        pl.when(lax.rem(r + nr - s, nr) == 0)(copy.wait_recv)
    for copy in u_copies[:sent]:
        copy.wait_send()
    for copy in u_copies[sent:]:
        copy.wait()
    for copy in mid_copies:
        copy.wait()

    right = uc[...]

    def update(q, carry):
        for i in range(per_dev):
            left = jnp.dot(
                mid_in[q, :, i * rmax : (i + 1) * rmax],
                ug[q, :, i * block : (i + 1) * block],
                preferred_element_type=F32,
            ).astype(BF16)
            rows = pl.ds(pl.multiple_of((q * per_dev + i) * block, block), block)
            base_ref[rows] = par[rows].astype(F32) - lax.dot_general(
                left, right, (((0,), (0,)), ((), ())), preferred_element_type=F32
            )
        return carry

    lax.fori_loop(0, nc, update, 0)

    for copy in pivot_1 + pivot_2:
        copy.wait_send()

    @pl.when(r == 0)
    def _():
        for copy in first_1:
            copy.wait_send()

    for copy in own:
        copy.wait()
    for copy in block_copies:
        copy.wait()


def add_kernel(cap, lab_ref, base_ref, arr_ref, out_ref, total, head, nxt, done):
    slots, block, _ = arr_ref.shape
    places = head.shape[0]

    def clear(i, carry):
        head[i] = -1
        return carry

    def link(j, carry):
        label = lab_ref[j // cap, 0, lax.rem(j, cap)]

        @pl.when(label >= 0)
        def _():
            nxt[j] = head[label]
            head[label] = j

        return carry

    lax.fori_loop(0, places, clear, 0)
    lax.fori_loop(0, slots, link, 0)

    def each(i, carry):
        rows = pl.ds(pl.multiple_of(i * block, block), block)
        first = head[i]

        @pl.when(first < 0)
        def _():
            pltpu.make_async_copy(base_ref.at[rows], out_ref.at[rows], done.at[i]).start()

        @pl.when(first >= 0)
        def _():
            total[rows] = base_ref[rows] + arr_ref[first].astype(F32)

            def add(j):
                total[rows] += arr_ref[j].astype(F32)
                return nxt[j]

            lax.while_loop(lambda j: j >= 0, add, nxt[first])
            pltpu.make_async_copy(total.at[rows], out_ref.at[rows], done.at[i]).start()

        return carry

    lax.fori_loop(0, places, each, 0)

    def finish(i, carry):
        rows = pl.ds(pl.multiple_of(i * block, block), block)
        pltpu.make_async_copy(total.at[rows], out_ref.at[rows], done.at[i]).wait()
        return carry

    lax.fori_loop(0, places, finish, 0)


def on_device(parent, contrib, owner, slot, pivot, u_factor, v_factor, rank):
    nr = lax.axis_size("row")
    nc = lax.axis_size("col")
    n = nr * nc
    held, block, _ = contrib.shape
    cap = max(2, (held + n - 1) // n)
    rmax = u_factor.shape[1]
    per_dev = rank.shape[0]
    half = block // 2
    slots = n * cap

    dma = pltpu.SemaphoreType.DMA
    vmem = pl.BlockSpec(memory_space=pltpu.VMEM)
    smem = pl.BlockSpec(memory_space=pltpu.SMEM)
    anywhere = pl.BlockSpec(memory_space=pl.ANY)
    arrived, in_labels, base = pl.pallas_call(
        functools.partial(exchange_kernel, nr, nc, cap, per_dev),
        out_shape=(
            jax.ShapeDtypeStruct((slots, block, block), contrib.dtype),
            jax.ShapeDtypeStruct((n, 1, 128), jnp.int32),
            jax.ShapeDtypeStruct(parent.shape, F32),
        ),
        in_specs=[smem] * 3 + [pl.BlockSpec(memory_space=pltpu.HBM)] * 5,
        out_specs=(anywhere, anywhere, vmem),
        scratch_shapes=[
            pltpu.VMEM(contrib.shape, contrib.dtype),
            pltpu.VMEM((slots, block, block), contrib.dtype),
            pltpu.VMEM((block, block), F32),
            pltpu.VMEM((rmax, per_dev * block), BF16),
            pltpu.VMEM((rmax, block), BF16),
            pltpu.VMEM((nc * rmax, block), BF16),
            pltpu.VMEM((nc, rmax, per_dev * block), BF16),
            pltpu.VMEM((rmax, block), BF16),
            pltpu.VMEM((nc * rmax, per_dev * rmax), BF16),
            pltpu.VMEM((nc, rmax, per_dev * rmax), BF16),
            pltpu.VMEM((n, 1, 128), jnp.int32),
            pltpu.VMEM(parent.shape, parent.dtype),
            pltpu.VMEM((half, half), F32),
            pltpu.VMEM((half, half), F32),
        ]
        + [dma((n,))] * 4
        + [dma((nc,))] * 8
        + [dma((nr,))] * 6
        + [dma((8,))],
        compiler_params=pltpu.CompilerParams(
            collective_id=0, has_side_effects=True, vmem_limit_bytes=28 << 20
        ),
    )(owner[:, 0], slot, rank, contrib, pivot, v_factor.T, u_factor.T, parent)

    places = parent.shape[0] // block
    return pl.pallas_call(
        functools.partial(add_kernel, cap),
        out_shape=jax.ShapeDtypeStruct(parent.shape, F32),
        in_specs=[smem, vmem, vmem],
        out_specs=anywhere,
        scratch_shapes=[
            pltpu.VMEM(parent.shape, F32),
            pltpu.SMEM((places,), jnp.int32),
            pltpu.SMEM((slots,), jnp.int32),
            dma((places,)),
        ],
        compiler_params=pltpu.CompilerParams(vmem_limit_bytes=24 << 20),
    )(in_labels, base, arrived)


def solution(mesh):
    in_specs = (
        P(("front", "row"), "col"),
        P(("front", "row", "col"), None, None),
        P(("front", "row", "col"), None),
        P(("front", "row", "col")),
        P(("front", "row", "col"), None),
        P(("front", "row", "col"), None),
        P(("front", "row", "col"), None),
        P(("front", "row", "col")),
    )
    return jax.shard_map(
        on_device, mesh=mesh, in_specs=in_specs, out_specs=P(("front", "row"), "col"), check_vma=False
    )
```

time: 150 us -> 134 us (0.89)
  the two profiles are of different devices: /device:TPU:0 before, /device:TPU:1 now
where the time goes in v2:
time: 134 us
  Pallas kernels  126 us (94%)
  local copies, waits for them, and re-layouts  8.46 us (6%)
    pallas_call x1, Pallas kernels, on_device(): pl.pallas_call(functools.partial(exchange_kernel, nr, nc, cap, per_dev),...  121 us
    unnamed x16, local copies, waits for them, and re-layouts  8.46 us
    pallas_call x1, Pallas kernels, on_device(): pl.pallas_call(functools.partial(add_kernel, cap), out_shape=jax.ShapeDty...  4.35 us

profile of v2, /device:TPU:1, one launch (start us, length us, event | category | flops | bytes accessed | tf_op | source)
XLA Modules:
  0.0 134.0 jit_solution(5973988053056338095)
XLA Ops:
  0.0 0.0 copy-start
  0.0 2.0 %copy-done = bf16[28,256,256]{2,1,0:T(8,128)(2,1)S(1)} copy-done((bf16[28,256,256]{2,1,0:T(8,128)(2,1)S(1)}, bf16[28,256,256]{2,1,0:T(8,128)(2,1)}, u32[]{:S(2)}) %copy-start) | copy-done | bytes 3670040
  2.0 0.0 copy-start.1
  2.0 1.9 %copy-done.1 = bf16[6144,256]{1,0:T(8,128)(2,1)S(1)} copy-done((bf16[6144,256]{1,0:T(8,128)(2,1)S(1)}, bf16[6144,256]{1,0:T(8,128)(2,1)}, u32[]{:S(2)}) %copy-start.1) | copy-done | bytes 3145752
  3.9 0.0 copy-start.2
  3.9 0.9 copy-done.2
  4.9 0.0 copy-start.3
  4.9 0.9 copy-done.3
  5.8 0.0 copy-start.4
  5.8 0.7 copy-done.4
  6.5 0.0 copy-start.5
  6.5 0.7 copy-done.5
  7.2 0.0 copy-start.6
  7.2 0.7 copy-done.6
  7.8 0.0 copy-start.7
  7.8 0.7 copy-done.7
  8.5 121.2 %shard_map.82 = (bf16[32,256,256]{2,1,0:T(8,128)(2,1)S(1)}, s32[16,1,128]{2,1,0:T(1,128)S(1)}, f32[6144,256]{1,0:T(8,128)S(1)}) custom-call(s32[28]{0:T(128)S(1)} %bitcast.5, s32[28]{0:T(128)S(1)} %copy-done.6, s32[6]{0:T(128)S(1)} %copy-done.7, bf16[28,256,256]{2,1,0:T(8,128)(2,1)S(1)} %copy-done, f32[16,256]{1,0:T(8,128)S(1)} %copy-done.4, ...), custom_call_target="tpu_custom_call" | custom-call | tf_op jit(solution)/shard_map/pallas_call | solution.py:389
  129.7 4.3 %shard_map.83 = f32[6144,256]{1,0:T(8,128)} custom-call(s32[16,1,128]{2,1,0:T(1,128)S(1)} %get-tuple-element.8.lab_ref, f32[6144,256]{1,0:T(8,128)S(1)} %get-tuple-element.9.base_ref, bf16[32,256,256]{2,1,0:T(8,128)(2,1)S(1)} %get-tuple-element.10.arr_ref), custom_call_target="tpu_custom_call" | custom-call | tf_op jit(solution)/shard_map/pallas_call | solution.py:424
Async XLA Ops:
  0.0 2.0 %copy-start = (bf16[28,256,256]{2,1,0:T(8,128)(2,1)S(1)}, bf16[28,256,256]{2,1,0:T(8,128)(2,1)}, u32[]{:S(2)}) copy-start(bf16[28,256,256]{2,1,0:T(8,128)(2,1)} %contrib_ref.1) | copy-start | bytes 11010052
  2.0 1.9 %copy-start.1 = (bf16[6144,256]{1,0:T(8,128)(2,1)S(1)}, bf16[6144,256]{1,0:T(8,128)(2,1)}, u32[]{:S(2)}) copy-start(bf16[6144,256]{1,0:T(8,128)(2,1)} %parent_ref.1) | copy-start | bytes 9437188
  3.9 0.9 copy-start.2
  4.9 0.9 copy-start.3
  5.8 0.7 copy-start.4
  6.5 0.7 copy-start.5
  7.2 0.7 copy-start.6
  7.8 0.7 copy-start.7

commit v3 on v2

--- a/solution.py
+++ b/solution.py
@@ -59,9 +59,9 @@
 
 def exchange_kernel(
     nr, nc, cap, per_dev,
-    owner_ref, slot_ref, rank_ref, contrib_ref, pivot_ref, vt_ref, ut_ref, parent_ref,
-    arr_ref, lab_ref, base_ref,
-    cbuf, pack, piv, vown, vfirst, vc, ug, uc, mid_out, mid_in, labels, par, work1, work2,
+    ints_ref, contrib_ref, pivot_ref, vt_ref, ut_ref,
+    arr_ref, lab_ref, term_ref,
+    cbuf, pack, piv, vown, vfirst, vc, ug, uc, mid_out, mid_in, labels, work1, work2,
     blk_s, blk_r, lab_s, lab_r, piv1_s, piv1_r, v1_s, v1_r, u_s, u_r, mid_s, mid_r,
     piv2_s, piv2_r, v2_s, v2_r, uc_s, uc_r, loc,
 ):
@@ -74,8 +74,11 @@
     rmax = vt_ref.shape[0]
     half = block // 2
 
+    wing = nc // 2
+
     def peer(s):
-        return lax.rem(r + s // nc, nr), lax.rem(c + s % nc, nc)
+        side = lax.rem(c // wing + (s % nc) // wing, 2)
+        return lax.rem(r + s // nc, nr), side * wing + lax.rem(lax.rem(c, wing) + s % wing, wing)
 
     def flip(m):
         return c + m - 2 * m * lax.rem(c // m, 2)
@@ -95,8 +98,7 @@
     load_contrib = pltpu.make_async_copy(contrib_ref, cbuf, loc.at[2])
     load_u = pltpu.make_async_copy(ut_ref, ug.at[c], loc.at[3])
     load_uc = pltpu.make_async_copy(first_u, uc, loc.at[4])
-    load_parent = pltpu.make_async_copy(parent_ref, par, loc.at[5])
-    for copy in (load_v, load_piv, load_contrib, load_u, load_parent):
+    for copy in (load_v, load_piv, load_contrib, load_u):
         copy.start()
     pl.when(r == 0)(load_uc.start)
 
@@ -106,7 +108,7 @@
         pl.semaphore_signal(barrier, inc=1, device_id={"row": rr, "col": cc}, device_id_type=MESH)
     load_v.wait()
     vfirst[...] = jnp.where(
-        lax.broadcasted_iota(jnp.int32, (rmax, block), 0) < rank_ref[0], vown[:, 0:block], 0
+        lax.broadcasted_iota(jnp.int32, (rmax, block), 0) < ints_ref[2 * held], vown[:, 0:block], 0
     ).astype(BF16)
     pl.semaphore_wait(barrier, n - 1)
 
@@ -153,7 +155,7 @@
 
         def look(j, carry):
             count, found = carry[0], carry[1:]
-            hit = owner_ref[j] == target
+            hit = ints_ref[j] == target
             found = [jnp.where(hit & (count == k), j, found[k]) for k in range(cap)]
             return (jnp.where(hit, count + 1, count), *found)
 
@@ -161,7 +163,7 @@
         row = jnp.full((1, 128), -1, jnp.int32)
         for k in range(cap):
             pack[s * cap + k] = cbuf[found[k]]
-            row = jnp.where(lane == k, jnp.where(count > k, slot_ref[found[k]], -1), row)
+            row = jnp.where(lane == k, jnp.where(count > k, ints_ref[held + found[k]], -1), row)
         labels[s] = row
 
     mine = arr_ref.at[pl.ds(me * cap, cap)]
@@ -177,7 +179,9 @@
             copy.start()
             block_copies.append(copy)
 
-    order = sorted(range(1, n), key=lambda s: (-min(s % nc, nc - s % nc), s // nc))
+    far = [s for s in range(1, n) if s % nc >= wing]
+    near = [s for s in range(1, n) if s % nc < wing]
+    order = [s for pair in zip(far, near + [0]) for s in pair if s]
     early = order[: (EARLY * len(order)) // 16]
     late = order[len(early) :]
     ahead = early[: nc // 2]
@@ -252,7 +256,7 @@
     parts = split3(inverse)
     place = lax.broadcasted_iota(jnp.int32, (rmax, block), 0)
     masked = [
-        jnp.where(place < rank_ref[i], vown[:, i * block : (i + 1) * block], 0).astype(BF16)
+        jnp.where(place < ints_ref[2 * held + i], vown[:, i * block : (i + 1) * block], 0).astype(BF16)
         for i in range(per_dev)
     ]
     g_own = solve(parts, jnp.concatenate(masked, axis=0))
@@ -276,7 +280,6 @@
     mid_in[c] = mid_out[pl.ds(pl.multiple_of(c * rmax, rmax), rmax)]
 
     load_u.wait()
-    load_parent.wait()
     pl.when(r == 0)(load_uc.wait)
     for s, copy in column_u:
         pl.when(r == 0)(copy.wait_send)
@@ -298,7 +301,7 @@
                 preferred_element_type=F32,
             ).astype(BF16)
             rows = pl.ds(pl.multiple_of((q * per_dev + i) * block, block), block)
-            base_ref[rows] = par[rows].astype(F32) - lax.dot_general(
+            term_ref[rows] = lax.dot_general(
                 left, right, (((0,), (0,)), ((), ())), preferred_element_type=F32
             )
         return carry
@@ -319,7 +322,7 @@
         copy.wait()
 
 
-def add_kernel(cap, lab_ref, base_ref, arr_ref, out_ref, total, head, nxt, done):
+def add_kernel(cap, lab_ref, parent_ref, term_ref, arr_ref, out_ref, total, head, nxt, done):
     slots, block, _ = arr_ref.shape
     places = head.shape[0]
 
@@ -346,18 +349,19 @@
 
         @pl.when(first < 0)
         def _():
-            pltpu.make_async_copy(base_ref.at[rows], out_ref.at[rows], done.at[i]).start()
+            total[rows] = parent_ref[rows].astype(F32) - term_ref[rows]
 
         @pl.when(first >= 0)
         def _():
-            total[rows] = base_ref[rows] + arr_ref[first].astype(F32)
+            total[rows] = parent_ref[rows].astype(F32) + arr_ref[first].astype(F32) - term_ref[rows]
 
             def add(j):
                 total[rows] += arr_ref[j].astype(F32)
                 return nxt[j]
 
             lax.while_loop(lambda j: j >= 0, add, nxt[first])
-            pltpu.make_async_copy(total.at[rows], out_ref.at[rows], done.at[i]).start()
+
+        pltpu.make_async_copy(total.at[rows], out_ref.at[rows], done.at[i]).start()
 
         return carry
 
@@ -386,14 +390,14 @@
     vmem = pl.BlockSpec(memory_space=pltpu.VMEM)
     smem = pl.BlockSpec(memory_space=pltpu.SMEM)
     anywhere = pl.BlockSpec(memory_space=pl.ANY)
-    arrived, in_labels, base = pl.pallas_call(
+    arrived, in_labels, term = pl.pallas_call(
         functools.partial(exchange_kernel, nr, nc, cap, per_dev),
         out_shape=(
             jax.ShapeDtypeStruct((slots, block, block), contrib.dtype),
             jax.ShapeDtypeStruct((n, 1, 128), jnp.int32),
             jax.ShapeDtypeStruct(parent.shape, F32),
         ),
-        in_specs=[smem] * 3 + [pl.BlockSpec(memory_space=pltpu.HBM)] * 5,
+        in_specs=[smem] + [anywhere] * 4,
         out_specs=(anywhere, anywhere, vmem),
         scratch_shapes=[
             pltpu.VMEM(contrib.shape, contrib.dtype),
@@ -407,7 +411,6 @@
             pltpu.VMEM((nc * rmax, per_dev * rmax), BF16),
             pltpu.VMEM((nc, rmax, per_dev * rmax), BF16),
             pltpu.VMEM((n, 1, 128), jnp.int32),
-            pltpu.VMEM(parent.shape, parent.dtype),
             pltpu.VMEM((half, half), F32),
             pltpu.VMEM((half, half), F32),
         ]
@@ -418,13 +421,13 @@
         compiler_params=pltpu.CompilerParams(
             collective_id=0, has_side_effects=True, vmem_limit_bytes=28 << 20
         ),
-    )(owner[:, 0], slot, rank, contrib, pivot, v_factor.T, u_factor.T, parent)
+    )(jnp.concatenate([owner[:, 0], slot, rank]), contrib, pivot, v_factor.T, u_factor.T)
 
     places = parent.shape[0] // block
     return pl.pallas_call(
         functools.partial(add_kernel, cap),
         out_shape=jax.ShapeDtypeStruct(parent.shape, F32),
-        in_specs=[smem, vmem, vmem],
+        in_specs=[smem, vmem, vmem, vmem],
         out_specs=anywhere,
         scratch_shapes=[
             pltpu.VMEM(parent.shape, F32),
@@ -433,7 +436,7 @@
             dma((places,)),
         ],
         compiler_params=pltpu.CompilerParams(vmem_limit_bytes=24 << 20),
-    )(in_labels, base, arrived)
+    )(in_labels, parent, term, arrived)
 
 
 def solution(mesh):

time: 134 us -> 123 us (0.918)
  the two profiles are of different devices: /device:TPU:1 before, /device:TPU:13 now
where the time goes in v3:
time: 123 us
  Pallas kernels  118 us (96%)
  local copies, waits for them, and re-layouts  4.61 us (4%)
    pallas_call x1, Pallas kernels, on_device(): pl.pallas_call(functools.partial(exchange_kernel, nr, nc, cap, per_dev),...  113 us
    unnamed x10, local copies, waits for them, and re-layouts  4.61 us
    pallas_call x1, Pallas kernels, on_device(): pl.pallas_call(functools.partial(add_kernel, cap), out_shape=jax.ShapeDty...  4.38 us

profile of v3, /device:TPU:13, one launch (start us, length us, event | category | flops | bytes accessed | tf_op | source)
XLA Modules:
  0.0 123.0 jit_solution(8472352626667169573)
XLA Ops:
  0.0 0.8 pad_add_fusion.ints_ref
  0.8 0.0 copy-start
  0.8 2.0 %copy-done = bf16[28,256,256]{2,1,0:T(8,128)(2,1)S(1)} copy-done((bf16[28,256,256]{2,1,0:T(8,128)(2,1)S(1)}, bf16[28,256,256]{2,1,0:T(8,128)(2,1)}, u32[]{:S(2)}) %copy-start) | copy-done | bytes 3670040
  2.8 0.0 copy-start.2
  2.8 0.9 copy-done.2
  3.7 0.0 copy-start.3
  3.7 0.9 copy-done.3
  4.7 0.0 copy-start.4
  4.7 0.7 copy-done.4
  5.4 0.0 copy-start.1
  5.4 113.2 %shard_map.82 = (bf16[32,256,256]{2,1,0:T(8,128)(2,1)S(1)}, s32[16,1,128]{2,1,0:T(1,128)S(1)}, f32[6144,256]{1,0:T(8,128)S(1)}) custom-call(s32[62]{0:T(128)S(1)} %pad_add_fusion.ints_ref, bf16[28,256,256]{2,1,0:T(8,128)(2,1)S(1)} %copy-done, f32[16,256]{1,0:T(8,128)S(1)} %copy-done.4, bf16[64,1536]{1,0:T(8,128)(2,1)S(1)} %bitcast.3, ...), custom_call_target="tpu_custom_call" | custom-call | tf_op jit(solution)/shard_map/pallas_call | solution.py:393
  118.6 0.0 copy-done.1
  118.6 4.4 %shard_map.83 = f32[6144,256]{1,0:T(8,128)} custom-call(s32[16,1,128]{2,1,0:T(1,128)S(1)} %get-tuple-element.8.lab_ref, bf16[6144,256]{1,0:T(8,128)(2,1)S(1)} %copy-done.1, f32[6144,256]{1,0:T(8,128)S(1)} %get-tuple-element.9.term_ref, bf16[32,256,256]{2,1,0:T(8,128)(2,1)S(1)} %get-tuple-element.10.arr_ref), custom_call_target="tpu_custom_call" | custom-call | tf_op jit(solution)/shard_map/pallas_call | solution.py:427
Async XLA Ops:
  0.8 2.0 %copy-start = (bf16[28,256,256]{2,1,0:T(8,128)(2,1)S(1)}, bf16[28,256,256]{2,1,0:T(8,128)(2,1)}, u32[]{:S(2)}) copy-start(bf16[28,256,256]{2,1,0:T(8,128)(2,1)} %contrib_ref.1) | copy-start | bytes 11010052
  2.8 0.9 copy-start.2
  3.7 0.9 copy-start.3
  4.7 0.7 copy-start.4
  5.4 113.2 %copy-start.1 = (bf16[6144,256]{1,0:T(8,128)(2,1)S(1)}, bf16[6144,256]{1,0:T(8,128)(2,1)}, u32[]{:S(2)}) copy-start(bf16[6144,256]{1,0:T(8,128)(2,1)} %parent_ref.1) | copy-start | bytes 9437188

commit v4 on v3

--- a/solution.py
+++ b/solution.py
@@ -59,9 +59,9 @@
 
 def exchange_kernel(
     nr, nc, cap, per_dev,
-    ints_ref, contrib_ref, pivot_ref, vt_ref, ut_ref,
+    ints_ref, contrib_ref, pivot_ref, both_ref,
     arr_ref, lab_ref, term_ref,
-    cbuf, pack, piv, vown, vfirst, vc, ug, uc, mid_out, mid_in, labels, work1, work2,
+    pack, piv, vfirst, vc, ug, uc, mid_out, mid_in, labels, work1, work2,
     blk_s, blk_r, lab_s, lab_r, piv1_s, piv1_r, v1_s, v1_r, u_s, u_r, mid_s, mid_r,
     piv2_s, piv2_r, v2_s, v2_r, uc_s, uc_r, loc,
 ):
@@ -71,7 +71,9 @@
     me = r * nc + c
     held, block, _ = contrib_ref.shape
     prows = pivot_ref.shape[0]
-    rmax = vt_ref.shape[0]
+    rmax = both_ref.shape[0] // 2
+    vt_ref = both_ref.at[pl.ds(0, rmax)]
+    ut_ref = both_ref.at[pl.ds(rmax, rmax)]
     half = block // 2
 
     wing = nc // 2
@@ -92,23 +94,18 @@
     my_piv = piv.at[pl.ds(pl.multiple_of(me * prows, prows), prows)]
     row_piv = piv.at[pl.ds(pl.multiple_of(r * nc * prows, nc * prows), nc * prows)]
     my_vc = vc.at[pl.ds(pl.multiple_of(c * rmax, rmax), rmax)]
-    first_u = ut_ref.at[:, pl.ds(0, block)]
-    load_v = pltpu.make_async_copy(vt_ref, vown, loc.at[0])
-    load_piv = pltpu.make_async_copy(pivot_ref, my_piv, loc.at[1])
-    load_contrib = pltpu.make_async_copy(contrib_ref, cbuf, loc.at[2])
-    load_u = pltpu.make_async_copy(ut_ref, ug.at[c], loc.at[3])
-    load_uc = pltpu.make_async_copy(first_u, uc, loc.at[4])
-    for copy in (load_v, load_piv, load_contrib, load_u):
-        copy.start()
-    pl.when(r == 0)(load_uc.start)
-
+    first_u = both_ref.at[pl.ds(rmax, rmax), pl.ds(0, block)]
+    load_u = pltpu.make_async_copy(ut_ref, ug.at[c], loc.at[0])
+    load_uc = pltpu.make_async_copy(first_u, uc, loc.at[1])
     barrier = pltpu.get_barrier_semaphore()
     for s in range(1, n):
         rr, cc = peer(s)
         pl.semaphore_signal(barrier, inc=1, device_id={"row": rr, "col": cc}, device_id_type=MESH)
-    load_v.wait()
+    load_u.start()
+    pl.when(r == 0)(load_uc.start)
+    piv[pl.ds(pl.multiple_of(me * prows, prows), prows)] = pivot_ref[...]
     vfirst[...] = jnp.where(
-        lax.broadcasted_iota(jnp.int32, (rmax, block), 0) < ints_ref[2 * held], vown[:, 0:block], 0
+        lax.broadcasted_iota(jnp.int32, (rmax, block), 0) < ints_ref[2 * held], vt_ref[:, 0:block], 0
     ).astype(BF16)
     pl.semaphore_wait(barrier, n - 1)
 
@@ -162,7 +159,7 @@
         count, *found = lax.fori_loop(0, held, look, (jnp.int32(0),) * (cap + 1))
         row = jnp.full((1, 128), -1, jnp.int32)
         for k in range(cap):
-            pack[s * cap + k] = cbuf[found[k]]
+            pack[s * cap + k] = contrib_ref[found[k]]
             row = jnp.where(lane == k, jnp.where(count > k, ints_ref[held + found[k]], -1), row)
         labels[s] = row
 
@@ -185,11 +182,9 @@
     early = order[: (EARLY * len(order)) // 16]
     late = order[len(early) :]
     ahead = early[: nc // 2]
-    load_contrib.wait()
     for s in ahead:
         pack_for(s)
 
-    load_piv.wait()
     for copy in pivot_1:
         copy.wait_recv()
     for s in range(1, nr):
@@ -221,8 +216,8 @@
     for s in late + [0]:
         pack_for(s)
     own = [
-        pltpu.make_async_copy(pack.at[pl.ds(0, cap)], mine, loc.at[6]),
-        pltpu.make_async_copy(labels.at[0], lab_ref.at[me], loc.at[7]),
+        pltpu.make_async_copy(pack.at[pl.ds(0, cap)], mine, loc.at[2]),
+        pltpu.make_async_copy(labels.at[0], lab_ref.at[me], loc.at[3]),
     ]
     for copy in own:
         copy.start()
@@ -256,7 +251,7 @@
     parts = split3(inverse)
     place = lax.broadcasted_iota(jnp.int32, (rmax, block), 0)
     masked = [
-        jnp.where(place < ints_ref[2 * held + i], vown[:, i * block : (i + 1) * block], 0).astype(BF16)
+        jnp.where(place < ints_ref[2 * held + i], vt_ref[:, i * block : (i + 1) * block], 0).astype(BF16)
         for i in range(per_dev)
     ]
     g_own = solve(parts, jnp.concatenate(masked, axis=0))
@@ -397,13 +392,11 @@
             jax.ShapeDtypeStruct((n, 1, 128), jnp.int32),
             jax.ShapeDtypeStruct(parent.shape, F32),
         ),
-        in_specs=[smem] + [anywhere] * 4,
+        in_specs=[smem, vmem, vmem, vmem],
         out_specs=(anywhere, anywhere, vmem),
         scratch_shapes=[
-            pltpu.VMEM(contrib.shape, contrib.dtype),
             pltpu.VMEM((slots, block, block), contrib.dtype),
             pltpu.VMEM((block, block), F32),
-            pltpu.VMEM((rmax, per_dev * block), BF16),
             pltpu.VMEM((rmax, block), BF16),
             pltpu.VMEM((nc * rmax, block), BF16),
             pltpu.VMEM((nc, rmax, per_dev * block), BF16),
@@ -417,11 +410,11 @@
         + [dma((n,))] * 4
         + [dma((nc,))] * 8
         + [dma((nr,))] * 6
-        + [dma((8,))],
+        + [dma((5,))],
         compiler_params=pltpu.CompilerParams(
             collective_id=0, has_side_effects=True, vmem_limit_bytes=28 << 20
         ),
-    )(jnp.concatenate([owner[:, 0], slot, rank]), contrib, pivot, v_factor.T, u_factor.T)
+    )(jnp.concatenate([owner[:, 0], slot, rank]), contrib, pivot, jnp.concatenate([v_factor.T, u_factor.T], axis=0))
 
     places = parent.shape[0] // block
     return pl.pallas_call(

time: 123 us -> 122 us (level)
  local copies, waits for them, and re-layouts: 4.61 us -> 2.75 us
    unnamed x10 -> x6, local copies, waits for them, and re-layouts: 4.61 us -> 2.75 us
where the time goes in v4:
time: 122 us; the launch traced here: 121 us
  Pallas kernels  117 us (96%)
  local copies, waits for them, and re-layouts  2.75 us (2%)
  other arithmetic  1.81 us (1%)
    pallas_call x1, Pallas kernels, on_device(): pl.pallas_call(functools.partial(exchange_kernel, nr, nc, cap, per_dev),...  112 us
    pallas_call x1, Pallas kernels, on_device(): pl.pallas_call(functools.partial(add_kernel, cap), out_shape=jax.ShapeDty...  4.33 us
    unnamed x6, local copies, waits for them, and re-layouts  2.75 us

profile of v4, /device:TPU:13, one launch (start us, length us, event | category | flops | bytes accessed | tf_op | source)
XLA Modules:
  0.0 121.3 jit_solution(11226475669019502128)
XLA Ops:
  0.0 0.8 pad_add_fusion.ints_ref
  0.8 1.0 pad_maximum_fusion.both_ref
  1.8 0.0 copy-start
  1.8 2.0 %copy-done = bf16[28,256,256]{2,1,0:T(8,128)(2,1)S(1)} copy-done((bf16[28,256,256]{2,1,0:T(8,128)(2,1)S(1)}, bf16[28,256,256]{2,1,0:T(8,128)(2,1)}, u32[]{:S(2)}) %copy-start) | copy-done | bytes 3670040
  3.9 0.0 copy-start.2
  3.9 0.7 copy-done.2
  4.6 0.0 copy-start.1
  4.6 112.4 %shard_map.82 = (bf16[32,256,256]{2,1,0:T(8,128)(2,1)S(1)}, s32[16,1,128]{2,1,0:T(1,128)S(1)}, f32[6144,256]{1,0:T(8,128)S(1)}) custom-call(s32[62]{0:T(128)S(1)} %pad_add_fusion.ints_ref, bf16[28,256,256]{2,1,0:T(8,128)(2,1)S(1)} %copy-done, f32[16,256]{1,0:T(8,128)S(1)} %copy-done.2, bf16[128,1536]{1,0:T(8,128)(2,1)S(1)} %pad_maximum_fusion.both_ref), custom_call_target="tpu_custom_call" | custom-call | tf_op jit(solution)/shard_map/pallas_call | solution.py:388
  117.0 0.0 copy-done.1
  117.0 4.3 %shard_map.83 = f32[6144,256]{1,0:T(8,128)} custom-call(s32[16,1,128]{2,1,0:T(1,128)S(1)} %get-tuple-element.8.lab_ref, bf16[6144,256]{1,0:T(8,128)(2,1)S(1)} %copy-done.1, f32[6144,256]{1,0:T(8,128)S(1)} %get-tuple-element.9.term_ref, bf16[32,256,256]{2,1,0:T(8,128)(2,1)S(1)} %get-tuple-element.10.arr_ref), custom_call_target="tpu_custom_call" | custom-call | tf_op jit(solution)/shard_map/pallas_call | solution.py:420
Async XLA Ops:
  1.8 2.0 %copy-start = (bf16[28,256,256]{2,1,0:T(8,128)(2,1)S(1)}, bf16[28,256,256]{2,1,0:T(8,128)(2,1)}, u32[]{:S(2)}) copy-start(bf16[28,256,256]{2,1,0:T(8,128)(2,1)} %contrib_ref.1) | copy-start | bytes 11010052
  3.9 0.7 copy-start.2
  4.6 112.4 %copy-start.1 = (bf16[6144,256]{1,0:T(8,128)(2,1)S(1)}, bf16[6144,256]{1,0:T(8,128)(2,1)}, u32[]{:S(2)}) copy-start(bf16[6144,256]{1,0:T(8,128)(2,1)} %parent_ref.1) | copy-start | bytes 9437188
